TPU v7x, 512 devices: a whole 4x8x8 slice. The times are simulated.
512 devices in a mesh: win: 32 (over x, y), seq: 16 (over z, core).
Axes of the slice: x: 4, y: 8, z: 8, core: 2. Of those that a mesh axis runs over, the one named last changes fastest.
Arguments:
- img_query: bfloat16 [128, 64, 2048], P('win', 'seq'), may hold values from -5 to 5, as said below
- img_key: bfloat16 [128, 64, 2048], P('win', 'seq'), may hold values from -5 to 5
- img_value: bfloat16 [128, 64, 2048], P('win', 'seq'), may hold values from -70 to 70
- text_kv: bfloat16 [2, 2, 512, 2048], P(None, None, None, 'seq'), may hold values from -6 to 6
- vel_weight: bfloat16 [2048, 64], P('seq'), may hold values from -0.125 to 0.125
- window_px: int32 [32], replicated, may hold values from 0 to 2032, as said below
Outputs:
- guided: float32 [128, 64, 64], P('win', 'seq')
Inputs may be any that keep to these rules, and one draw needn't show every extreme that they name: `img_query`: queries and keys lie within the range. `window_px`: multiples of 16. Taken in increasing order, the k-th offset lies in [16 k * 4, 16 (k + 1) * 4) for k = 0 to 31; the smallest is 0 and the largest 16 (127).
All inputs are finite; a program needn't handle non-finite values.
Results may differ from a plain program's by a relative error of at most 0.0031.
Values may be sent and summed in bfloat16 or wider, within the bound.
A program may use at most 64 MiB of HBM per device.

v0:
```python
import math

import jax
import jax.numpy as jnp
from jax import lax
from jax.sharding import PartitionSpec as P

HD = 128
HEADS = 16
LAT = 64
TXT = 512
WIN_ROWS = 32
WIN_COLS = 64


clip_rms = 0.3
guide_scale = 5.0
tiny = 1e-06


def attend_block(queries, img_keys, img_values, text_pair):
    inv_root = 1.0 / math.sqrt(queries.shape[-1])
    own_scores = jnp.dot(queries, img_keys.T, preferred_element_type=jnp.float32) * inv_root
    own_max = jnp.max(own_scores, axis=1, keepdims=True)
    results = []
    for branch in range(2):
        text_scores = (
            jnp.dot(queries, text_pair[branch, 0].T, preferred_element_type=jnp.float32) * inv_root
        )
        row_max = jnp.maximum(own_max, jnp.max(text_scores, axis=1, keepdims=True))
        own_exp = jnp.exp(own_scores - row_max)
        text_exp = jnp.exp(text_scores - row_max)
        denom_sum = jnp.sum(own_exp, axis=1, keepdims=True) + jnp.sum(
            text_exp, axis=1, keepdims=True
        )
        own_prob = (own_exp / denom_sum).astype(jnp.bfloat16)
        text_prob = (text_exp / denom_sum).astype(jnp.bfloat16)
        mixture = jnp.dot(own_prob, img_values, preferred_element_type=jnp.float32)
        mixture = mixture + jnp.dot(
            text_prob, text_pair[branch, 1], preferred_element_type=jnp.float32
        )
        results.append(mixture.astype(jnp.bfloat16))
    return jnp.stack(results, axis=1)


def local(img_query, img_key, img_value, text_kv, vel_weight, window_px):
    rows_dev = img_query.shape[0]
    cols_dev = img_query.shape[1]
    win_count = lax.axis_size("win")
    rows_all = rows_dev * win_count
    my_group = lax.axis_index("win")
    starts = window_px // 16
    picker = jnp.arange(starts.shape[0], dtype=jnp.int32) == my_group
    my_start = jnp.sum(jnp.where(picker, starts, 0))
    whole_cols = (
        lax.all_gather(img_query, "win", axis=0, tiled=True),
        lax.all_gather(img_key, "win", axis=0, tiled=True),
        lax.all_gather(img_value, "win", axis=0, tiled=True),
    )
    window_slabs = [
        jnp.roll(column_part, -my_start, axis=0)[:WIN_ROWS] for column_part in whole_cols
    ]

    def column_major(slab_rows):
        return jnp.transpose(slab_rows, (1, 0, 2)).reshape(cols_dev, WIN_ROWS, HEADS, HD)

    spread = (
        lax.all_to_all(
            column_major(window_slabs[0]), "seq", split_axis=2, concat_axis=0, tiled=True
        ),
        lax.all_to_all(
            column_major(window_slabs[1]), "seq", split_axis=2, concat_axis=0, tiled=True
        ),
        lax.all_to_all(
            column_major(window_slabs[2]), "seq", split_axis=2, concat_axis=0, tiled=True
        ),
    )
    heads_dev = HEADS // lax.axis_size("seq")
    tok_count = WIN_COLS * WIN_ROWS
    block_rows = math.gcd(tok_count, 512)
    query_heads = jnp.moveaxis(spread[0].reshape(tok_count, heads_dev, HD), 1, 0)
    key_heads = jnp.moveaxis(spread[1].reshape(tok_count, heads_dev, HD), 1, 0)
    value_heads = jnp.moveaxis(spread[2].reshape(tok_count, heads_dev, HD), 1, 0)
    text_heads = jnp.moveaxis(text_kv.reshape(2, 2, TXT, heads_dev, HD), 3, 0)

    def one_head(packed):
        queries, img_keys, img_values, text_pair = packed
        blocks = queries.reshape(tok_count // block_rows, block_rows, HD)

        def run_block(query_rows):
            return attend_block(query_rows, img_keys, img_values, text_pair)

        return lax.map(run_block, blocks).reshape(tok_count, 2, HD)

    attn_out = lax.map(one_head, (query_heads, key_heads, value_heads, text_heads))
    attn_cols = jnp.transpose(attn_out, (1, 2, 0, 3)).reshape(WIN_COLS, WIN_ROWS, 2, heads_dev * HD)
    flat_rows = attn_cols.reshape(cols_dev * lax.axis_size("seq") * WIN_ROWS * 2, heads_dev * HD)
    window_vel = lax.psum_scatter(
        jnp.dot(flat_rows, vel_weight, preferred_element_type=jnp.float32).reshape(
            cols_dev * lax.axis_size("seq"), WIN_ROWS, 2 * LAT
        ),
        "seq",
        scatter_dimension=0,
        tiled=True,
    )
    vel_rows = jnp.transpose(window_vel, (1, 0, 2))
    padded = jnp.concatenate(
        [vel_rows, jnp.zeros((rows_all - WIN_ROWS, cols_dev, 2 * LAT), jnp.float32)], axis=0
    )
    placed = jnp.roll(padded, my_start, axis=0)
    canvas_sum = lax.psum_scatter(placed, "win", scatter_dimension=0, tiled=True)
    own_rows = my_group * rows_dev + jnp.arange(rows_dev, dtype=jnp.int32)
    covered = jnp.mod(own_rows[:, None] - starts[None, :], rows_all) < WIN_ROWS
    counts = jnp.sum(covered.astype(jnp.int32), axis=1)
    canvas_vel = canvas_sum / counts.astype(jnp.float32)[:, None, None]
    cond_vel = canvas_vel[:, :, :LAT]
    delta_vel = cond_vel - canvas_vel[:, :, LAT:]
    totals = lax.psum(
        (
            jnp.sum(delta_vel * delta_vel),
            jnp.sum(delta_vel * cond_vel),
            jnp.sum(cond_vel * cond_vel),
        ),
        ("win", "seq"),
    )
    clip_limit = clip_rms * math.sqrt(rows_all * WIN_COLS * LAT)
    clip_factor = jnp.minimum(1.0, clip_limit / jnp.sqrt(totals[0] + tiny))
    along_cond = totals[1] / (totals[2] + tiny)
    return cond_vel + (guide_scale - 1.0) * clip_factor * (delta_vel - along_cond * cond_vel)


def solution(mesh):
    in_specs = (
        P("win", "seq", None),
        P("win", "seq", None),
        P("win", "seq", None),
        P(None, None, None, "seq"),
        P("seq", None),
        P(),
    )
    out_specs = P("win", "seq", None)
    return jax.shard_map(local, mesh=mesh, in_specs=in_specs, out_specs=out_specs, check_vma=False)
```

profile of v0, /device:TPU:1, one launch (start us, length us, event | category | flops | bytes accessed | tf_op | source)
XLA Modules:
  0.0 641.5 jit_solution(10433889727552998486)
XLA Ops:
  8.7 1.3 fusion.38
  11.4 84.2 %all-gather.4.cloned.1.call-done = bf16[128,4,2048]{2,1,0:T(4,128)(2,1)} async-done(((bf16[4,4,2048]{2,1,0:T(4,128)(2,1)}), bf16[128,4,2048]{2,1,0:T(4,128)(2,1)}) %all-gather.4.cloned.1.call-update) | async-done | bytes 2097168 | tf_op jit(solution)/shard_map/all_gather | solution.py:56
  95.6 2.4 copy_bitcast_fusion.2
  98.0 11.8 %all-to-all-start = ((bf16[4,32,16,128]{3,0,1,2:T(4,128)(2,1)}), bf16[4,32,16,128]{3,0,1,2:T(4,128)(2,1)S(1)}, u32[]{:S(2)}, u32[]{:S(2)}) async-start(bf16[4,32,16,128]{3,0,1,2:T(4,128)(2,1)} %copy_bitcast_fusion.2), calls=%async_computation | async-start | bytes 1048576 | tf_op jit(solution)/shard_map/all_to_all | solution.py:68
  109.8 69.7 %all-gather.6.cloned.1.call-done = bf16[128,4,2048]{2,1,0:T(4,128)(2,1)} async-done(((bf16[4,4,2048]{2,1,0:T(4,128)(2,1)}), bf16[128,4,2048]{2,1,0:T(4,128)(2,1)}) %all-gather.6.cloned.1.call-update) | async-done | bytes 2097168 | tf_op jit(solution)/shard_map/all_gather | solution.py:57
  179.5 2.4 copy_bitcast_fusion.1
  181.9 12.0 %all-to-all-start.1 = ((bf16[4,32,16,128]{3,0,1,2:T(4,128)(2,1)}), bf16[4,32,16,128]{3,0,1,2:T(4,128)(2,1)S(1)}, u32[]{:S(2)}, u32[]{:S(2)}) async-start(bf16[4,32,16,128]{3,0,1,2:T(4,128)(2,1)} %copy_bitcast_fusion.1), calls=%async_computation.1 | async-start | bytes 1048576 | tf_op jit(solution)/shard_map/all_to_all | solution.py:71
  193.9 69.6 %all-gather.8.cloned.1.call-done = bf16[128,4,2048]{2,1,0:T(4,128)(2,1)} async-done(((bf16[4,4,2048]{2,1,0:T(4,128)(2,1)}), bf16[128,4,2048]{2,1,0:T(4,128)(2,1)}) %all-gather.8.cloned.1.call-update) | async-done | bytes 2097168 | tf_op jit(solution)/shard_map/all_gather | solution.py:58
  263.5 2.4 copy_bitcast_fusion
  265.9 11.8 %all-to-all-start.2 = ((bf16[4,32,16,128]{3,0,1,2:T(4,128)(2,1)}), bf16[4,32,16,128]{3,0,1,2:T(4,128)(2,1)S(1)}, u32[]{:S(2)}, u32[]{:S(2)}) async-start(bf16[4,32,16,128]{3,0,1,2:T(4,128)(2,1)} %copy_bitcast_fusion), calls=%async_computation.2 | async-start | bytes 1048576 | tf_op jit(solution)/shard_map/all_to_all | solution.py:74
  278.0 17.0 %all-to-all-done.2 = bf16[4,32,16,128]{3,0,1,2:T(4,128)(2,1)S(1)} async-done(((bf16[4,32,16,128]{3,0,1,2:T(4,128)(2,1)}), bf16[4,32,16,128]{3,0,1,2:T(4,128)(2,1)S(1)}, u32[]{:S(2)}, u32[]{:S(2)}) %all-to-all-start.2) | async-done | bytes 524320 | tf_op jit(solution)/shard_map/all_to_all | solution.py:74
  295.2 26.3 %while.17 = (s32[]{:T(128)}, bf16[4,512,2,128]{3,2,1,0:T(2,128)(2,1)}, bf16[4,512,128]{2,1,0:T(8,128)(2,1)S(1)}, bf16[2048,128]{1,0:T(8,128)(2,1)S(1)}, bf16[2,2...) while((s32[]{:T(128)}, bf16[4,512,2,128]{3,2,1,0:T(2,128)(2,1)}, ...), condition=%wide.region_9.11_spmd, body=%wide.region_1.10_spmd.sunk | while | flops 1090386432 | bytes 27980376 | solution.py:93
  296.9 1.3 fusion.76
  298.2 0.9 fusion.80
  300.8 1.0 copy_dynamic-update-slice_fusion.2
  303.5 1.3 fusion.76
  304.8 0.9 fusion.80
  307.4 1.0 copy_dynamic-update-slice_fusion.2
  310.1 1.3 fusion.76
  311.3 0.9 fusion.80
  313.9 1.0 copy_dynamic-update-slice_fusion.2
  316.6 1.3 fusion.76
  317.9 0.9 fusion.80
  320.5 1.0 copy_dynamic-update-slice_fusion.2
  321.5 1.6 fusion.43
  323.1 1.3 reshape.65
  325.8 48.9 %reduce-scatter.2.cloned.1.call-done = f32[4,32,128]{2,1,0:T(8,128)} async-done(((f32[64,32,128]{2,1,0:T(8,128)}), f32[4,32,128]{2,1,0:T(8,128)}) %reduce-scatter.2.cloned.1.call-update) | async-done | bytes 65552 | tf_op jit(solution)/shard_map/reduce_scatter | solution.py:98
  374.8 0.9 copy.49
  375.7 1.4 fusion.35
  377.4 1.3 dynamic-slice.1
  379.3 150.7 %all-reduce.4.cloned.1.call-done = f32[128,4,128]{2,1,0:T(4,128)} async-done(((f32[128,4,128]{2,1,0:T(4,128)}), f32[128,4,128]{2,1,0:T(4,128)}) %all-reduce.4.cloned.1.call-update) | async-done | bytes 262160
  531.6 100.7 %all-reduce.1 = (f32[]{:T(128)}, f32[]{:T(128)}, f32[]{:T(128)}) all-reduce(f32[]{:T(128)} %get-tuple-element.61, f32[]{:T(128)} %get-tuple-element.60, f32[]{:T(128)} %get-tuple-element.59), channel_id=1, replica_groups=mesh['win'=32,'seq'=16] {'win','seq'}, use_global_device_ids=true, to_apply=%region_16.18 | all-reduce | flops 3 | bytes 24 | tf_op jit(solution)/shard_map/psum | solution.py:118
  (71 shorter events, 18.7 us)
Async XLA Ops:
  6.5 314.9 %copy-start = (bf16[128,64]{0,1:T(8,128)(2,1)S(1)}, bf16[128,64]{0,1:T(8,128)(2,1)}, u32[]{:S(2)}) copy-start(bf16[128,64]{0,1:T(8,128)(2,1)} %param.14) | copy-start | bytes 49156
  6.5 89.1 %all-gather.4.cloned.1.call-start = ((), (), s32[]{:S(2)}) async-start(), calls=%async_computation.4 | async-start | bytes 2162688 | tf_op jit(solution)/shard_map/all_gather | solution.py:56
  7.3 172.3 %all-gather.6.cloned.1.call-start = ((), (), s32[]{:S(2)}) async-start(), calls=%async_computation.5 | async-start | bytes 2162688 | tf_op jit(solution)/shard_map/all_gather | solution.py:57
  8.0 255.5 %all-gather.8.cloned.1.call-start = ((), (), s32[]{:S(2)}) async-start(), calls=%async_computation.6 | async-start | bytes 2162688 | tf_op jit(solution)/shard_map/all_gather | solution.py:58
  98.0 83.9 %all-to-all-start = ((bf16[4,32,16,128]{3,0,1,2:T(4,128)(2,1)}), bf16[4,32,16,128]{3,0,1,2:T(4,128)(2,1)S(1)}, u32[]{:S(2)}, u32[]{:S(2)}) async-start(bf16[4,32,16,128]{3,0,1,2:T(4,128)(2,1)} %copy_bitcast_fusion.2), calls=%async_computation | async-start | bytes 1048576 | tf_op jit(solution)/shard_map/all_to_all | solution.py:68
  181.9 113.2 %copy-start.1 = (bf16[2,2,512,128]{3,2,1,0:T(8,128)(2,1)S(1)}, bf16[2,2,512,128]{3,2,1,0:T(8,128)(2,1)}, u32[]{:S(2)}) copy-start(bf16[2,2,512,128]{3,2,1,0:T(8,128)(2,1)} %param.13) | copy-start | bytes 1572868
  181.9 84.0 %all-to-all-start.1 = ((bf16[4,32,16,128]{3,0,1,2:T(4,128)(2,1)}), bf16[4,32,16,128]{3,0,1,2:T(4,128)(2,1)S(1)}, u32[]{:S(2)}, u32[]{:S(2)}) async-start(bf16[4,32,16,128]{3,0,1,2:T(4,128)(2,1)} %copy_bitcast_fusion.1), calls=%async_computation.1 | async-start | bytes 1048576 | tf_op jit(solution)/shard_map/all_to_all | solution.py:71
  265.9 29.1 %all-to-all-start.2 = ((bf16[4,32,16,128]{3,0,1,2:T(4,128)(2,1)}), bf16[4,32,16,128]{3,0,1,2:T(4,128)(2,1)S(1)}, u32[]{:S(2)}, u32[]{:S(2)}) async-start(bf16[4,32,16,128]{3,0,1,2:T(4,128)(2,1)} %copy_bitcast_fusion), calls=%async_computation.2 | async-start | bytes 1048576 | tf_op jit(solution)/shard_map/all_to_all | solution.py:74
  277.7 97.1 %reduce-scatter.2.cloned.1.call-start = ((), (), s32[]{:S(2)}) async-start(), calls=%async_computation.7 | async-start | bytes 1114112 | tf_op jit(solution)/shard_map/reduce_scatter | solution.py:98
  324.5 205.6 %all-reduce.4.cloned.1.call-start = ((), (), s32[]{:S(2)}) async-start(), calls=%async_computation.8 | async-start | bytes 524288
Sparse Core Ops, SparseCore 0:
  10.5 85.0 all-gather.3
  98.8 80.7 all-gather.5
  182.7 80.7 all-gather.7
  324.6 50.1 reduce-scatter.1
  378.5 151.5 all-reduce.3
where the time goes:
time: 642 us; the launch traced here: 641 us
  waiting for transfers between devices  442 us (69%)
  blocking collectives  101 us (16%)
  starting transfers between devices  35.8 us (6%)
  other arithmetic  18.8 us (3%)
  between operations  18.5 us (3%)
  matrix products  17.4 us (3%)
  local copies, waits for them, and re-layouts  7.77 us (1%)
    unnamed x6, waiting for transfers between devices  153 us
    psum x1, blocking collectives, local(): lax.psum((jnp.sum(delta_vel * delta_vel), jnp.sum(delta_vel * cond_vel),...  101 us
    all_gather x1, waiting for transfers between devices, local(): lax.all_gather(img_query, 'win', axis=0, tiled=True)  84.2 us
    all_gather x1, waiting for transfers between devices, local(): lax.all_gather(img_key, 'win', axis=0, tiled=True)  69.7 us
    all_gather x1, waiting for transfers between devices, local(): lax.all_gather(img_value, 'win', axis=0, tiled=True)  69.6 us
    reduce_scatter x1, waiting for transfers between devices, local(): lax.psum_scatter(jnp.dot(flat_rows, vel_weight, preferred_element_type=jn...  48.9 us
    all_to_all x1, waiting for transfers between devices, local(): lax.all_to_all(column_major(window_slabs[2]), 'seq', split_axis=2, concat...  17 us
  transfers between devices with their start and end apart: 8, of which 6 were waited for; matrix products, arithmetic and copies ran while one was open for 2% of the time, Pallas kernels for 0%

commit v1 on v0

v1 whole, which is shorter than its diff:
```python
import math

import jax
import jax.numpy as jnp
from jax import lax
from jax.experimental import pallas as pl
from jax.experimental.pallas import tpu as pltpu
from jax.sharding import PartitionSpec as P

HD = 128
HEADS = 16
LAT = 64
TXT = 512
ROWS = 128
WIN_COLS = 64
WINDOWS = 32
SEQ = 16
OWN = 16
TOK = SEQ * OWN

clip_rms = 0.3
guide_scale = 5.0
tiny = 1e-06

SC = math.log2(math.e) / math.sqrt(HD)
LOW = -1e30
FLOOR = -1e29
MESH = pl.DeviceIdType.MESH
f32 = jnp.float32
bf16 = jnp.bfloat16


def mod(value, n):
    return lax.rem(value, jnp.int32(n))


def div(value, n):
    return lax.div(value, jnp.int32(n))


def pick(index, options):
    out = jnp.int32(options[0])
    for n, option in enumerate(options[1:], 1):
        out = jnp.where(index == n, jnp.int32(option), out)
    return out


class Place:
    def __init__(self):
        self.w = w = lax.axis_index("win")
        self.s = s = lax.axis_index("seq")
        self.x, self.y = div(w, 8), mod(w, 8)
        self.p, self.a = div(self.y, 2), mod(self.y, 2)
        self.z, self.c = div(s, 2), mod(s, 2)
        self.base = 8 * self.x + 2 * self.p
        self.block = self.base + self.c
        self.home = 4 * self.x + self.p
        self.head = 2 * self.z + self.a
        self.own_copy = self.c == self.a
        self.me = 2 * self.home + self.c

    def dest(self, d):
        zd, ad = mod(self.z + div(d, 2), SEQ // 2), mod(self.a + mod(d, 2), 2)
        return {"win": self.base + ad, "seq": 2 * zd + self.a}, 2 * zd + ad

    def source(self, d):
        seq = mod(self.s + d, SEQ)
        return {"win": self.base + self.c, "seq": seq}, seq

    def peer(self, g):
        n = mod(self.me + g, 32)
        pair, core = div(n, 2), mod(n, 2)
        return {"win": 8 * div(pair, 4) + 2 * mod(pair, 4) + self.a, "seq": 2 * self.z + core}

    def ring_of(self, j):
        turn = pick(j, (0, 3, 1, 0, 0, 2, 3, 1, 2))
        pp = mod(self.p + turn, 4)
        side = jnp.where(j == 3, 1, jnp.where(j == 4, 3, jnp.where(pp < self.p, 1, 3)))
        far = (j == 3) | (j == 4) | (j >= 6)
        xx = jnp.where(far, mod(self.x + side, 4), self.x)
        place = pp - self.p + 4
        place = jnp.where(far, jnp.where(side == 1, place + 4, place - 4), place)
        return pp, 4 * xx + pp, place

    def send_all(self, copy, keep):
        @pl.when(self.own_copy)
        def _():
            keep().start()

        @pl.when(jnp.logical_not(self.own_copy))
        def _():
            copy(jnp.int32(0)).start()

        @pl.loop(1, SEQ)
        def _(d):
            copy(d).start()


def remote(src, dst, send, recv, to):
    return pltpu.make_async_remote_copy(
        src_ref=src, dst_ref=dst, send_sem=send, recv_sem=recv, device_id=to, device_id_type=MESH
    )


def await_bytes(ref, sem):
    pltpu.make_async_copy(ref, ref, sem).wait()


def hello(to):
    pl.semaphore_signal(pltpu.get_barrier_semaphore(), inc=1, device_id=to, device_id_type=MESH)


def greet_heads(at):
    @pl.loop(1, SEQ)
    def _(d):
        hello(at.dest(d)[0])
        hello(at.source(d)[0])

    @pl.when(jnp.logical_not(at.own_copy))
    def _():
        hello(at.dest(jnp.int32(0))[0])
        hello(at.source(jnp.int32(0))[0])


def collect(
    q_in, k_in, v_in, text_in, wt_in, kv, q_buf, text, wt,
    raw, stage, l_in, s_own, r_own, s_blk, s_sib, r_blk, r_sib, s_text, r_text,
):
    at = Place()
    w, s, x, y, p, a, z, c = at.w, at.s, at.x, at.y, at.p, at.a, at.z, at.c
    home, head, own_copy = at.home, at.head, at.own_copy
    loads = [pltpu.make_async_copy(ref, raw.at[n], l_in.at[n]) for n, ref in enumerate((k_in, v_in, q_in))]
    for load in loads:
        load.start()

    greet_heads(at)
    sibling = {"win": w, "seq": 2 * z + 1 - c}
    up = {"win": 8 * x + 2 * mod(p + 1, 4) + a, "seq": s}
    down = {"win": 8 * x + 2 * mod(p + 3, 4) + a, "seq": s}
    hello(sibling)
    hello(up)
    hello(down)
    hello({"win": 8 * mod(x + 1, 4) + y, "seq": s})
    hello({"win": 8 * mod(x + 3, 4) + y, "seq": s})

    for n, load in enumerate(loads):
        load.wait()
        flat = raw[n].reshape(OWN, HEADS * HD)
        for h in range(HEADS):
            stage[n, h] = flat[:, h * HD : (h + 1) * HD]

    pl.semaphore_wait(pltpu.get_barrier_semaphore(), jnp.where(own_copy, 2 * SEQ + 3, 2 * SEQ + 5))

    rows = pl.ds(pl.multiple_of(OWN * s, OWN), OWN)
    for n in range(3):
        dst = q_buf.at[rows, :] if n == 2 else kv.at[home, a, n, rows, :]

        def give(d, n=n, dst=dst):
            to, h = at.dest(d)
            return remote(stage.at[n, h], dst, s_own.at[0], r_own.at[n], to)

        def keep(n=n, dst=dst):
            return pltpu.make_async_copy(stage.at[n, head], dst, r_own.at[n])

        at.send_all(give, keep)


    def text_sends():
        return (
            remote(text_in, text, s_text.at[0], r_text.at[0], sibling),
            remote(wt_in, wt, s_text.at[1], r_text.at[1], sibling),
        )

    @pl.when(own_copy)
    def _():
        pltpu.make_async_copy(text_in, text, r_text.at[0]).start()
        pltpu.make_async_copy(wt_in, wt, r_text.at[1]).start()
        for copy in text_sends():
            copy.start()

    def blk(pair, core, n):
        return kv.at[pair, core, n]

    def send_block(n, pair, step, to, sem):
        remote(blk(pair, c, n), blk(pair, c, n), s_blk.at[sem, n], r_blk.at[step, n], to).start()

    def send_x(n, pair, step, side):
        send_block(n, pair, step, {"win": 8 * mod(x + side, 4) + y, "seq": s}, step)

    def send_sib(n, pair, step):
        remote(blk(pair, c, n), blk(pair, c, n), s_sib.at[step, n], r_sib.at[step, n], sibling).start()

    def arrived(n, pair, step):
        await_bytes(blk(pair, c, n), r_blk.at[step, n])

    def hand_on(n, step, x_step):
        pp, pair, _ = at.ring_of(jnp.int32(step))
        arrived(n, pair, step)
        if step == 1 and n == 0:
            send_block(n, pair, 5, up, 5)
        if step == 2 and n == 1:
            send_block(n, pair, 5, down, 5)
        send_x(n, pair, x_step, jnp.where(pp < p, 3, 1))
        send_sib(n, pair, step)

    await_bytes(blk(home, c, 0), r_own.at[0])
    send_block(0, home, 1, up, 1)
    send_x(0, home, 4, 1)
    send_x(0, home, 3, 3)
    send_sib(0, home, 0)
    await_bytes(blk(home, c, 1), r_own.at[1])
    send_block(1, home, 2, down, 2)
    send_block(1, home, 1, up, 1)
    send_block(0, home, 2, down, 2)
    send_x(1, home, 4, 1)
    send_x(1, home, 3, 3)
    send_sib(1, home, 0)
    await_bytes(q_buf, r_own.at[2])

    @pl.loop(0, 9)
    def _(j):
        _, pair, _ = at.ring_of(j)

        @pl.when(j == 1)
        def _():
            hand_on(0, 1, 6)
            hand_on(1, 2, 7)
            hand_on(1, 1, 6)
            hand_on(0, 2, 7)

        @pl.when(j == 5)
        def _():
            hand_on(0, 5, 8)
            hand_on(1, 5, 8)

        @pl.when((j == 3) | (j == 4) | (j >= 6))
        def _():
            for n in range(2):
                arrived(n, pair, j)
                send_sib(n, pair, j)

    @pl.loop(0, 9)
    def _(j):
        _, pair, _ = at.ring_of(j)
        for n in range(2):
            await_bytes(blk(pair, 1 - c, n), r_sib.at[j, n])

    for n in range(2):
        await_bytes((text, wt)[n], r_text.at[n])

    @pl.when(own_copy)
    def _():
        for copy in text_sends():
            copy.wait_send()
        await_bytes(stage.at[:, pl.ds(0, SEQ - 1)], s_own.at[0])

    @pl.when(jnp.logical_not(own_copy))
    def _():
        await_bytes(stage, s_own.at[0])

    @pl.loop(0, 9)
    def _(j):
        for n in range(2):
            await_bytes(blk(home, c, n), s_sib.at[j, n])

        @pl.when(j > 0)
        def _():
            for n in range(2):
                await_bytes(blk(home, c, n), s_blk.at[j, n])


def mix(
    q_buf, kv, text, wt, px, vel, qt_buf, part, top, low, ptext, coef, attn, starts,
):
    at = Place()
    block, c = at.block, at.c

    def scan_start(n, found):
        start = div(px[n], 16)
        slot = div(start, 4)
        off = start - 4 * slot
        return tuple(
            old + jnp.where(slot == mod(block + 24 + i, 32), off, 0) for i, old in enumerate(found)
        )

    offsets = lax.fori_loop(0, WINDOWS, scan_start, (jnp.int32(0),) * 9)
    for i in range(9):
        starts[i] = offsets[i]

    qt_buf[...] = q_buf[...].T

    def segment(scores, values_t):
        peak = jnp.maximum(jnp.max(scores, axis=0, keepdims=True), FLOOR)
        weights = jnp.exp2((scores - peak) * SC)
        total = jnp.sum(weights, axis=0, keepdims=True)
        return peak, total, jnp.dot(values_t, weights.astype(bf16), preferred_element_type=f32)

    def attend(pair, core, place):
        b = 2 * place + core - c
        scores = jnp.dot(kv[pair, core, 0], qt_buf[...], preferred_element_type=f32)
        values_t = kv[pair, core, 1].T
        key_row = mod(div(lax.broadcasted_iota(jnp.int32, (TOK, 1), 0), 4), 4)

        def keep(kind, masked):
            peak, total, mix = segment(masked, values_t)
            row = b + 1
            top[kind, pl.ds(row, 1), :] = peak
            low[kind, pl.ds(row, 1), :] = total
            part[kind, row] = mix

        keep(0, scores)
        begins = b <= 8
        bound = starts[jnp.clip(jnp.where(begins, b, b - 8), 0, 8)]
        first = jnp.where(begins, bound, 0)
        last = jnp.where(begins, 4, bound)
        inside = (key_row >= first) & (key_row < last)
        keep(1, scores + jnp.where(inside, 0.0, LOW))

        @pl.when(b == 8)
        def _():
            peak, total, mix = segment(scores + jnp.where(key_row < starts[0], 0.0, LOW), values_t)
            top[2, 0:1, :] = peak
            low[2, 0:1, :] = total
            part[2, 0] = mix

    @pl.loop(0, 2)
    def _(branch):
        scores = jnp.dot(text[branch, 0], qt_buf[...], preferred_element_type=f32)
        peak, total, mix = segment(scores, text[branch, 1].T)
        top[2, pl.ds(8 + branch, 1), :] = peak
        low[2, pl.ds(8 + branch, 1), :] = total
        ptext[branch] = mix

    @pl.loop(0, 9)
    def _(j):
        pair = mod(at.home + 12 + j, 16)
        attend(pair, 0, j)
        attend(pair, 1, j)

    query_row = mod(div(lax.broadcasted_iota(jnp.int32, (1, TOK), 1), 4), 4)
    holds_first = (query_row < starts[0]).astype(f32)
    holds_last = (query_row >= starts[8]).astype(f32)
    share = 1.0 / (7.0 + holds_first + holds_last)
    which = lax.broadcasted_iota(jnp.int32, (9, TOK), 0)
    member = jnp.where(which == 0, holds_first * share, jnp.where(which == 8, holds_last * share, share))

    head_top, head_low = top[1, 1:10, :], low[1, 1:10, :]
    tail_top = jnp.concatenate([top[2, 0:1, :], top[1, 10:18, :]], axis=0)
    tail_low = jnp.concatenate([low[2, 0:1, :], low[1, 10:18, :]], axis=0)
    peak = jnp.maximum(head_top, tail_top)
    for d in range(1, 8):
        peak = jnp.maximum(peak, top[0, 1 + d : 10 + d, :])
    e_head = jnp.exp2((head_top - peak) * SC)
    e_tail = jnp.exp2((tail_top - peak) * SC)
    total = e_head * head_low + e_tail * tail_low
    e_full = []
    for d in range(1, 8):
        e_full.append(jnp.exp2((top[0, 1 + d : 10 + d, :] - peak) * SC))
        total = total + e_full[-1] * low[0, 1 + d : 10 + d, :]
    coef[...] = jnp.zeros_like(coef)
    for branch in range(2):
        text_top, text_low = top[2, 8 + branch : 9 + branch, :], low[2, 8 + branch : 9 + branch, :]
        both = jnp.maximum(peak, text_top)
        e_img = jnp.exp2((peak - both) * SC)
        e_text = jnp.exp2((text_top - both) * SC)
        scale = member / (e_img * total + e_text * text_low)
        gain = e_img * scale
        for d in range(1, 8):
            coef[branch, 0, 1 + d : 10 + d, :] += gain * e_full[d - 1]
        coef[branch, 1, 1:10, :] = gain * e_head
        coef[branch, 2, 0:9, :] = gain * e_tail
        coef[branch, 2, 9:10, :] = jnp.sum(e_text * scale, axis=0, keepdims=True)

    @pl.loop(0, 8)
    def _(chunk):
        feats = pl.ds(pl.multiple_of(chunk * 16, 16), 16)
        sums = [jnp.zeros((16, TOK), f32), jnp.zeros((16, TOK), f32)]

        def add(value, kind, row):
            for branch in range(2):
                sums[branch] = sums[branch] + value * coef[branch, kind, row : row + 1, :]

        for b in range(1, 16):
            add(part[0, b + 1, feats, :], 0, b + 1)
        for b in range(0, 9):
            add(part[1, b + 1, feats, :], 1, b + 1)
        add(part[2, 0, feats, :], 2, 0)
        for b in range(9, 17):
            add(part[1, b + 1, feats, :], 2, b - 8)
        for branch in range(2):
            mixed = sums[branch] + ptext[branch, feats, :] * coef[branch, 2, 9:10, :]
            main = mixed.astype(bf16)
            attn[pl.ds(pl.multiple_of(branch * HD + chunk * 16, 16), 16), :] = main
            attn[pl.ds(pl.multiple_of((2 + branch) * HD + chunk * 16, 16), 16), :] = (
                mixed - main.astype(f32)
            ).astype(bf16)

    proj = wt[...]
    proj = jnp.concatenate(
        [
            jnp.concatenate([proj, jnp.zeros_like(proj)], axis=1),
            jnp.concatenate([proj, -proj], axis=1),
        ],
        axis=0,
    )
    proj = jnp.concatenate([proj, proj], axis=1)
    vel[...] = jnp.dot(proj, attn[...], preferred_element_type=f32).T.astype(bf16)


def finish(vel, out_ref, rs, st, st2, ar1, ar2, s_sum, r_sum):
    at = Place()
    s, head, me, own_copy = at.s, at.head, at.me, at.own_copy
    rows = pl.ds(pl.multiple_of(OWN * s, OWN), OWN)
    greet_heads(at)

    @pl.loop(1, 32)
    def _(g):
        hello(at.peer(g))

    pl.semaphore_wait(pltpu.get_barrier_semaphore(), jnp.where(own_copy, 2 * SEQ + 29, 2 * SEQ + 31))

    def rs_copy(d):
        to, seq = at.source(d)
        there = pl.ds(pl.multiple_of(OWN * seq, OWN), OWN)
        return remote(vel.at[there, :], rs.at[head], s_sum.at[0], r_sum.at[0], to)

    at.send_all(rs_copy, lambda: pltpu.make_async_copy(vel.at[rows, :], rs.at[head], r_sum.at[0]))
    await_bytes(rs, r_sum.at[0])

    mine = jnp.sum(rs[...].astype(f32), axis=0)
    turned = pltpu.roll(mine, LAT, 1)
    st[...] = jnp.concatenate(
        [jnp.sum(mine * mine, axis=0, keepdims=True), jnp.sum(mine * turned, axis=0, keepdims=True)], axis=0
    )

    def a1_copy(d):
        return remote(st, ar1.at[s], s_sum.at[1], r_sum.at[1], at.dest(d)[0])

    at.send_all(a1_copy, lambda: pltpu.make_async_copy(st, ar1.at[s], r_sum.at[1]))
    await_bytes(ar1, r_sum.at[1])
    st2[...] = jnp.sum(ar1[...], axis=0)

    @pl.loop(1, 32)
    def _(g):
        remote(st2, ar2.at[me], s_sum.at[2], r_sum.at[2], at.peer(g)).start()

    pltpu.make_async_copy(st2, ar2.at[me], r_sum.at[2]).start()
    await_bytes(ar2, r_sum.at[2])
    sums = jnp.sum(ar2[...], axis=0)
    is_cond = lax.broadcasted_iota(jnp.int32, (1, 2 * LAT), 1) < LAT
    s_cc = jnp.sum(jnp.where(is_cond, sums[0:1, :], 0.0), axis=1, keepdims=True)
    s_dd = jnp.sum(jnp.where(is_cond, 0.0, sums[0:1, :]), axis=1, keepdims=True)
    s_dc = jnp.sum(jnp.where(is_cond, sums[1:2, :], 0.0), axis=1, keepdims=True)
    clip_limit = clip_rms * math.sqrt(ROWS * WIN_COLS * LAT)
    clip_factor = jnp.minimum(1.0, clip_limit / jnp.sqrt(s_dd + tiny))
    along = s_dc / (s_cc + tiny)
    guided = mine + (guide_scale - 1.0) * clip_factor * (turned - along * mine)
    out_ref[...] = guided[:, :LAT]

    @pl.when(own_copy)
    def _():
        await_bytes(rs.at[pl.ds(0, SEQ - 1)], s_sum.at[0])
        await_bytes(ar1.at[pl.ds(0, SEQ - 1)], s_sum.at[1])

    @pl.when(jnp.logical_not(own_copy))
    def _():
        await_bytes(rs, s_sum.at[0])
        await_bytes(ar1, s_sum.at[1])

    await_bytes(ar2.at[pl.ds(0, 31)], s_sum.at[2])


def local(img_query, img_key, img_value, text_kv, vel_weight, window_px):
    dma = pltpu.SemaphoreType.DMA
    vmem = pl.BlockSpec(memory_space=pltpu.VMEM)
    kv, queries, text, wt = pl.pallas_call(
        collect,
        out_shape=[
            jax.ShapeDtypeStruct((16, 2, 2, TOK, HD), bf16),
            jax.ShapeDtypeStruct((TOK, HD), bf16),
            jax.ShapeDtypeStruct((2, 2, TXT, HD), bf16),
            jax.ShapeDtypeStruct((LAT, HD), bf16),
        ],
        in_specs=[pl.BlockSpec(memory_space=pltpu.HBM)] * 5,
        out_specs=[vmem] * 4,
        scratch_shapes=[
            pltpu.VMEM((3, 4, 4, HEADS * HD), bf16),
            pltpu.VMEM((3, HEADS, OWN, HD), bf16),
            dma((3,)),
            dma((1,)),
            dma((3,)),
            dma((9, 2)),
            dma((9, 2)),
            dma((9, 2)),
            dma((9, 2)),
            dma((2,)),
            dma((2,)),
        ],
        compiler_params=pltpu.CompilerParams(collective_id=0, has_side_effects=True, vmem_limit_bytes=16 * 2**20),
    )(img_query, img_key, img_value, text_kv, vel_weight.T)
    vel = pl.pallas_call(
        mix,
        out_shape=jax.ShapeDtypeStruct((TOK, 2 * LAT), bf16),
        in_specs=[vmem] * 4 + [pl.BlockSpec(memory_space=pltpu.SMEM)],
        out_specs=vmem,
        scratch_shapes=[
            pltpu.VMEM((HD, TOK), bf16),
            pltpu.VMEM((3, 19, HD, TOK), f32),
            pltpu.VMEM((3, 24, TOK), f32),
            pltpu.VMEM((3, 24, TOK), f32),
            pltpu.VMEM((2, HD, TOK), f32),
            pltpu.VMEM((2, 3, 24, TOK), f32),
            pltpu.VMEM((4 * HD, TOK), bf16),
            pltpu.SMEM((9,), jnp.int32),
        ],
        compiler_params=pltpu.CompilerParams(vmem_limit_bytes=24 * 2**20),
    )(queries, kv, text, wt, window_px)
    out = pl.pallas_call(
        finish,
        out_shape=jax.ShapeDtypeStruct((OWN, LAT), f32),
        in_specs=[vmem],
        out_specs=vmem,
        scratch_shapes=[
            pltpu.VMEM((HEADS, OWN, 2 * LAT), bf16),
            pltpu.VMEM((2, 2 * LAT), f32),
            pltpu.VMEM((2, 2 * LAT), f32),
            pltpu.VMEM((SEQ, 2, 2 * LAT), f32),
            pltpu.VMEM((32, 2, 2 * LAT), f32),
            dma((3,)),
            dma((3,)),
        ],
        compiler_params=pltpu.CompilerParams(collective_id=1, has_side_effects=True),
    )(vel)
    return out.reshape(4, 4, LAT)


def solution(mesh):
    in_specs = (
        P("win", "seq", None),
        P("win", "seq", None),
        P("win", "seq", None),
        P(None, None, None, "seq"),
        P("seq", None),
        P(),
    )
    out_specs = P("win", "seq", None)
    return jax.shard_map(local, mesh=mesh, in_specs=in_specs, out_specs=out_specs, check_vma=False)
```

time: 642 us -> 84.4 us (0.13)
  waiting for transfers between devices: 442 us -> 0 us
  blocking collectives: 101 us -> 0 us
  Pallas kernels: 0 us -> 77.1 us
  starting transfers between devices: 35.8 us -> 0 us
  other arithmetic: 18.8 us -> 0 us
  between operations: 18.5 us -> 0.04 us
  matrix products: 17.4 us -> 0 us
    all_gather x3 -> x0, waiting for transfers between devices: 224 us -> none  [the longest x1 84.2 us: local(): lax.all_gather(img_query, 'win', axis=0, tiled=True)]
    unnamed x6 -> x0, waiting for transfers between devices: 153 us -> none
    psum x1 -> x0, blocking collectives: 101 us -> none  [local(): lax.psum((jnp.sum(delta_vel * delta_vel), jnp.sum(delta_vel * cond_vel),...]
    pallas_call x0 -> x3, Pallas kernels: none -> 77.1 us  [the longest x1 40.3 us: local(): pl.pallas_call(collect, out_shape=[jax.ShapeDtypeStruct((16, 2, 2, TOK, H...]
    reduce_scatter x1 -> x0, waiting for transfers between devices: 48.9 us -> none  [local(): lax.psum_scatter(jnp.dot(flat_rows, vel_weight, preferred_element_type=jn...]
    all_to_all x3 -> x0, starting transfers between devices: 35.6 us -> none  [the longest x1 12 us: local(): lax.all_to_all(column_major(window_slabs[1]), 'seq', split_axis=2, concat...]
    dot_general x29 -> x0, matrix products: 17.4 us -> none  [the longest x8 7.02 us: attend_block(): mixture = jnp.dot(own_prob, img_values, preferred_element_type=jnp.float32)]
    all_to_all x3 -> x0, waiting for transfers between devices: 17 us -> none  [the longest x1 17 us: local(): lax.all_to_all(column_major(window_slabs[2]), 'seq', split_axis=2, concat...]
  transfers between devices with their start and end apart: 8 -> 0, of which waited for: 6 -> 0; matrix products, arithmetic and copies ran while one was open for 2% -> 0% of each run, Pallas kernels for 0% -> 0%
where the time goes in v1:
time: 84.4 us; the launch traced here: 84 us
  Pallas kernels  77.1 us (91%)
  local copies, waits for them, and re-layouts  6.84 us (8%)
    pallas_call x1, Pallas kernels, local(): pl.pallas_call(collect, out_shape=[jax.ShapeDtypeStruct((16, 2, 2, TOK, H...  40.3 us
    pallas_call x1, Pallas kernels, local(): pl.pallas_call(finish, out_shape=jax.ShapeDtypeStruct((OWN, LAT), f32), i...  23.9 us
    pallas_call x1, Pallas kernels, local(): pl.pallas_call(mix, out_shape=jax.ShapeDtypeStruct((TOK, 2 * LAT), bf16),...  13 us
    unnamed x15, local copies, waits for them, and re-layouts  6.84 us

profile of v1, /device:TPU:1, one launch (start us, length us, event | category | flops | bytes accessed | tf_op | source)
XLA Modules:
  0.0 84.0 jit_solution(6493800378671176380)
XLA Ops:
  0.0 0.0 copy-start
  0.0 1.0 %copy-done = bf16[2,2,512,128]{3,2,1,0:T(8,128)(2,1)S(1)} copy-done((bf16[2,2,512,128]{3,2,1,0:T(8,128)(2,1)S(1)}, bf16[2,2,512,128]{3,2,1,0:T(8,128)(2,1)}, u32[]{:S(2)}) %copy-start) | copy-done | bytes 524312
  1.0 0.0 copy-start.2
  1.0 0.8 copy-done.2
  1.9 0.0 copy-start.3
  1.9 0.8 copy-done.3
  2.7 0.0 copy-start.4
  2.7 0.8 copy-done.4
  3.6 0.0 copy-start.5
  3.6 0.7 copy-done.5
  4.3 40.3 %shard_map.64 = (bf16[16,2,2,256,128]{4,3,2,1,0:T(8,128)(2,1)S(1)}, bf16[256,128]{1,0:T(8,128)(2,1)S(1)}, bf16[2,2,512,128]{3,2,1,0:T(8,128)(2,1)S(1)}, bf16[64,128]{1,0:T(8,128)(2,1)S(1)}) custom-call(bf16[4,4,2048]{2,1,0:T(4,128)(2,1)S(1)} %copy-done.2, bf16[4,4,2048]{2,1,0:T(4,128)(2,1)S(1)} %copy-done.3, bf16[4,4,2048]{2,1,0:T(4,128)(2,1)S(1)} %copy-done.4, ...), custom_call_target="tpu_custom_call" | custom-call | tf_op jit(solution)/shard_map/pallas_call | solution.py:476
  44.6 0.0 copy-start.6
  44.6 0.6 copy-done.6
  45.2 13.0 %shard_map.65.vel = bf16[256,128]{1,0:T(8,128)(2,1)S(1)} custom-call(bf16[256,128]{1,0:T(8,128)(2,1)S(1)} %get-tuple-element.9.q_buf, bf16[16,2,2,256,128]{4,3,2,1,0:T(8,128)(2,1)S(1)} %get-tuple-element.10.kv, bf16[2,2,512,128]{3,2,1,0:T(8,128)(2,1)S(1)} %get-tuple-element.11.text, bf16[64,128]{1,0:T(8,128)(2,1)S(1)} %get-tuple-element.12.wt, s32[32]{0:T(128)S(1)} %copy-done.6), custom_call_target="tpu_custom_call" | custom-call | tf_op jit(solution)/shard_map/pallas_call | solution.py:501
  58.2 0.0 copy-start.1
  58.2 0.6 copy-done.1
  58.8 23.9 %shard_map.66 = f32[16,64]{1,0:T(8,128)} custom-call(bf16[256,128]{1,0:T(8,128)(2,1)} %copy-done.1), custom_call_target="tpu_custom_call" | custom-call | tf_op jit(solution)/shard_map/pallas_call | solution.py:518
  82.7 1.3 %copy.8 = f32[4,4,64]{2,1,0:T(4,128)} copy(f32[4,4,64]{2,1,0:T(4,128)} %bitcast.3) | data formatting | bytes 8192
Async XLA Ops:
  0.0 1.0 %copy-start = (bf16[2,2,512,128]{3,2,1,0:T(8,128)(2,1)S(1)}, bf16[2,2,512,128]{3,2,1,0:T(8,128)(2,1)}, u32[]{:S(2)}) copy-start(bf16[2,2,512,128]{3,2,1,0:T(8,128)(2,1)} %text_in.1) | copy-start | bytes 1572868
  1.0 0.8 copy-start.2
  1.9 0.8 copy-start.3
  2.7 0.8 copy-start.4
  3.6 0.7 copy-start.5
  44.6 0.7 copy-start.6
  58.2 0.6 copy-start.1

commit v2 on v1

v2 whole, which is shorter than its diff:
```python
import math

import jax
import jax.numpy as jnp
from jax import lax
from jax.experimental import pallas as pl
from jax.experimental.pallas import tpu as pltpu
from jax.sharding import PartitionSpec as P

HD = 128
HEADS = 16
LAT = 64
TXT = 512
ROWS = 128
WIN_COLS = 64
WINDOWS = 32
SEQ = 16
OWN = 16
TOK = SEQ * OWN

clip_rms = 0.3
guide_scale = 5.0
tiny = 1e-06

SC = math.log2(math.e) / math.sqrt(HD)
LOW = -1e30
FLOOR = -1e29
MESH = pl.DeviceIdType.MESH
f32 = jnp.float32
bf16 = jnp.bfloat16


def mod(value, n):
    return lax.rem(value, jnp.int32(n))


def div(value, n):
    return lax.div(value, jnp.int32(n))


def pick(index, options):
    out = jnp.int32(options[0])
    for n, option in enumerate(options[1:], 1):
        out = jnp.where(index == n, jnp.int32(option), out)
    return out


def kernel(
    q_in, k_in, v_in, text_in, wt_in, px, out_ref,
    raw, stage, kvd, kvs, q_buf, qt_buf, text, wt, part, top, low, ptext, coef, attn, vel, rs, st, st2, ar1, ar2, starts,
    l_in, s_own, r_own, s_blk, s_sib, r_blk, r_sib, s_text, r_text, s_sum, r_sum,
):
    w = lax.axis_index("win")
    s = lax.axis_index("seq")
    x, y = div(w, 8), mod(w, 8)
    p, a = div(y, 2), mod(y, 2)
    z, c = div(s, 2), mod(s, 2)
    base = 8 * x + 2 * p
    block = base + c
    home = 4 * x + p
    head = 2 * z + a
    own_copy = c == a
    zero = jnp.int32(0)

    def dest(d):
        zd, ad = mod(z + div(d, 2), SEQ // 2), mod(a + mod(d, 2), 2)
        return {"win": base + ad, "seq": 2 * zd + a}, 2 * zd + ad

    def source(d):
        return {"win": base + c, "seq": mod(s + d, SEQ)}, mod(s + d, SEQ)

    def along_seq(d):
        return {"win": w, "seq": mod(s + d, SEQ)}

    def along_win(g):
        return {"win": mod(w + g, 32), "seq": s}

    def remote(src, dst, send, recv, to):
        return pltpu.make_async_remote_copy(
            src_ref=src, dst_ref=dst, send_sem=send, recv_sem=recv, device_id=to, device_id_type=MESH
        )

    def await_bytes(ref, sem):
        pltpu.make_async_copy(ref, ref, sem).wait()

    def send_all(copy, keep):
        @pl.when(own_copy)
        def _():
            keep().start()

        @pl.when(jnp.logical_not(own_copy))
        def _():
            copy(zero).start()

        @pl.loop(1, SEQ)
        def _(d):
            copy(d).start()

    loads = [pltpu.make_async_copy(ref, raw.at[n], l_in.at[n]) for n, ref in enumerate((k_in, v_in, q_in))]
    for load in loads:
        load.start()

    barrier = pltpu.get_barrier_semaphore()

    def hello(to):
        pl.semaphore_signal(barrier, inc=1, device_id=to, device_id_type=MESH)

    @pl.loop(1, SEQ)
    def _(d):
        hello(dest(d)[0])
        hello(source(d)[0])
        hello(along_seq(d))

    @pl.when(jnp.logical_not(own_copy))
    def _():
        hello(dest(zero)[0])
        hello(source(zero)[0])

    @pl.loop(1, 32)
    def _(g):
        hello(along_win(g))

    rows = pl.ds(pl.multiple_of(OWN * s, OWN), OWN)
    for n, load in enumerate(loads):
        load.wait()
        flat = raw[n].reshape(OWN, HEADS * HD)
        for h in range(HEADS):
            stage[n, h] = flat[:, h * HD : (h + 1) * HD]
        if n == 0:
            pl.semaphore_wait(barrier, jnp.where(own_copy, 3 * SEQ + 28, 3 * SEQ + 30))
        dst = q_buf.at[rows, :] if n == 2 else kvd.at[0, n, rows, :]

        def give(d, n=n, dst=dst):
            to, h = dest(d)
            return remote(stage.at[n, h], dst, s_own.at[0], r_own.at[n], to)

        def keep(n=n, dst=dst):
            return pltpu.make_async_copy(stage.at[n, head], dst, r_own.at[n])

        send_all(give, keep)

    sibling = {"win": w, "seq": 2 * z + 1 - c}

    def text_sends():
        return (
            remote(text_in, text, s_text.at[0], r_text.at[0], sibling),
            remote(wt_in, wt, s_text.at[1], r_text.at[1], sibling),
        )

    @pl.when(own_copy)
    def _():
        pltpu.make_async_copy(text_in, text, r_text.at[0]).start()
        pltpu.make_async_copy(wt_in, wt, r_text.at[1]).start()
        for copy in text_sends():
            copy.start()

    def place_of(j):
        turn = pick(j, (0, 3, 1, 0, 0, 2, 3, 1, 2))
        pp = mod(p + turn, 4)
        side = jnp.where(j == 3, 1, jnp.where(j == 4, 3, jnp.where(pp < p, 1, 3)))
        far = (j == 3) | (j == 4) | (j >= 6)
        place = pp - p + 4
        place = jnp.where(far, jnp.where(side == 1, place + 4, place - 4), place)
        return place

    up = {"win": 8 * x + 2 * mod(p + 1, 4) + a, "seq": s}
    down = {"win": 8 * x + 2 * mod(p + 3, 4) + a, "seq": s}

    def send_block(n, have, step, to):
        remote(kvd.at[have, n], kvd.at[step, n], s_blk.at[step, n], r_blk.at[step, n], to).start()

    def send_x(n, have, step, side):
        send_block(n, have, step, {"win": 8 * mod(x + side, 4) + y, "seq": s})

    def send_sib(n, step):
        remote(kvd.at[step, n], kvs.at[step, n], s_sib.at[step, n], r_sib.at[step, n], sibling).start()

    def hand_on(n, step, turn, x_step):
        await_bytes(kvd.at[step, n], r_blk.at[step, n])
        if step == 1 and n == 0:
            send_block(n, step, 5, up)
        if step == 2 and n == 1:
            send_block(n, step, 5, down)
        send_x(n, step, x_step, jnp.where(mod(p + turn, 4) < p, 3, 1))
        send_sib(n, step)

    await_bytes(kvd.at[0, 0], r_own.at[0])
    send_block(0, 0, 1, up)
    send_x(0, 0, 4, 1)
    send_x(0, 0, 3, 3)
    send_sib(0, 0)
    await_bytes(kvd.at[0, 1], r_own.at[1])
    send_block(1, 0, 2, down)
    send_block(1, 0, 1, up)
    send_block(0, 0, 2, down)
    send_x(1, 0, 4, 1)
    send_x(1, 0, 3, 3)
    send_sib(1, 0)
    def scan_start(n, found):
        start = div(px[n], 16)
        slot = div(start, 4)
        off = start - 4 * slot
        return tuple(
            old + jnp.where(slot == mod(block + 24 + i, 32), off, 0) for i, old in enumerate(found)
        )

    offsets = lax.fori_loop(0, WINDOWS, scan_start, (zero,) * 9)
    for i in range(9):
        starts[i] = offsets[i]

    await_bytes(q_buf, r_own.at[2])

    qt_buf[...] = q_buf[...].T

    def segment(scores, values_t):
        peak = jnp.maximum(jnp.max(scores, axis=0, keepdims=True), FLOOR)
        weights = jnp.exp2((scores - peak) * SC)
        total = jnp.sum(weights, axis=0, keepdims=True)
        return peak, total, jnp.dot(values_t, weights.astype(bf16), preferred_element_type=f32)

    def attend(held, j, core, place):
        b = 2 * place + core - c
        scores = jnp.dot(held[j, 0], qt_buf[...], preferred_element_type=f32)
        values_t = held[j, 1].T
        key_row = mod(div(lax.broadcasted_iota(jnp.int32, (TOK, 1), 0), 4), 4)

        def keep(kind, masked):
            peak, total, mix = segment(masked, values_t)
            row = b + 1
            top[kind, pl.ds(row, 1), :] = peak
            low[kind, pl.ds(row, 1), :] = total
            part[kind, row] = mix

        keep(0, scores)
        begins = b <= 8
        bound = starts[jnp.clip(jnp.where(begins, b, b - 8), 0, 8)]
        first = jnp.where(begins, bound, 0)
        last = jnp.where(begins, 4, bound)
        inside = (key_row >= first) & (key_row < last)
        keep(1, scores + jnp.where(inside, 0.0, LOW))

        @pl.when(b == 8)
        def _():
            peak, total, mix = segment(scores + jnp.where(key_row < starts[0], 0.0, LOW), values_t)
            top[2, 0:1, :] = peak
            low[2, 0:1, :] = total
            part[2, 0] = mix

    def text_part():
        for n in range(2):
            pltpu.make_async_copy((text_in, wt_in)[n], (text, wt)[n], r_text.at[n]).wait()

        @pl.loop(0, 2)
        def _(branch):
            scores = jnp.dot(text[branch, 0], qt_buf[...], preferred_element_type=f32)
            peak, total, mix = segment(scores, text[branch, 1].T)
            top[2, pl.ds(8 + branch, 1), :] = peak
            low[2, pl.ds(8 + branch, 1), :] = total
            ptext[branch] = mix

    @pl.loop(0, 9)
    def _(j):
        place = place_of(j)

        def pass_on(step):
            for n in range(2):
                await_bytes(kvd.at[step, n], r_blk.at[step, n])
                send_sib(n, step)

        @pl.when(j == 1)
        def _():
            hand_on(0, 1, 3, 6)
            hand_on(1, 2, 1, 7)
            hand_on(1, 1, 3, 6)
            hand_on(0, 2, 1, 7)
            pass_on(3)
            pass_on(4)

        @pl.when(j == 3)
        def _():
            hand_on(0, 5, 2, 8)
            hand_on(1, 5, 2, 8)

        @pl.when(j == 5)
        def _():
            pass_on(6)
            pass_on(7)

        @pl.when(j == 8)
        def _():
            pass_on(8)

        attend(kvd, j, c, place)

        @pl.when(j == 0)
        def _():
            text_part()

        for n in range(2):
            await_bytes(kvs.at[j, n], r_sib.at[j, n])
        attend(kvs, j, 1 - c, place)

    query_row = mod(div(lax.broadcasted_iota(jnp.int32, (1, TOK), 1), 4), 4)
    holds_first = (query_row < starts[0]).astype(f32)
    holds_last = (query_row >= starts[8]).astype(f32)
    share = 1.0 / (7.0 + holds_first + holds_last)
    which = lax.broadcasted_iota(jnp.int32, (9, TOK), 0)
    member = jnp.where(which == 0, holds_first * share, jnp.where(which == 8, holds_last * share, share))

    head_top, head_low = top[1, 1:10, :], low[1, 1:10, :]
    tail_top = jnp.concatenate([top[2, 0:1, :], top[1, 10:18, :]], axis=0)
    tail_low = jnp.concatenate([low[2, 0:1, :], low[1, 10:18, :]], axis=0)
    peak = jnp.maximum(head_top, tail_top)
    for d in range(1, 8):
        peak = jnp.maximum(peak, top[0, 1 + d : 10 + d, :])
    e_head = jnp.exp2((head_top - peak) * SC)
    e_tail = jnp.exp2((tail_top - peak) * SC)
    total = e_head * head_low + e_tail * tail_low
    e_full = []
    for d in range(1, 8):
        e_full.append(jnp.exp2((top[0, 1 + d : 10 + d, :] - peak) * SC))
        total = total + e_full[-1] * low[0, 1 + d : 10 + d, :]
    coef[...] = jnp.zeros_like(coef)
    for branch in range(2):
        text_top, text_low = top[2, 8 + branch : 9 + branch, :], low[2, 8 + branch : 9 + branch, :]
        both = jnp.maximum(peak, text_top)
        e_img = jnp.exp2((peak - both) * SC)
        e_text = jnp.exp2((text_top - both) * SC)
        scale = member / (e_img * total + e_text * text_low)
        gain = e_img * scale
        for d in range(1, 8):
            coef[branch, 0, 1 + d : 10 + d, :] += gain * e_full[d - 1]
        coef[branch, 1, 1:10, :] = gain * e_head
        coef[branch, 2, 0:9, :] = gain * e_tail
        coef[branch, 2, 9:10, :] = jnp.sum(e_text * scale, axis=0, keepdims=True)

    @pl.loop(0, 8)
    def _(chunk):
        feats = pl.ds(pl.multiple_of(chunk * 16, 16), 16)
        sums = [jnp.zeros((16, TOK), f32), jnp.zeros((16, TOK), f32)]

        def add(value, kind, row):
            for branch in range(2):
                sums[branch] = sums[branch] + value * coef[branch, kind, row : row + 1, :]

        for b in range(1, 16):
            add(part[0, b + 1, feats, :], 0, b + 1)
        for b in range(0, 9):
            add(part[1, b + 1, feats, :], 1, b + 1)
        add(part[2, 0, feats, :], 2, 0)
        for b in range(9, 17):
            add(part[1, b + 1, feats, :], 2, b - 8)
        for branch in range(2):
            mixed = sums[branch] + ptext[branch, feats, :] * coef[branch, 2, 9:10, :]
            main = mixed.astype(bf16)
            attn[pl.ds(pl.multiple_of(branch * HD + chunk * 16, 16), 16), :] = main
            attn[pl.ds(pl.multiple_of((2 + branch) * HD + chunk * 16, 16), 16), :] = (
                mixed - main.astype(f32)
            ).astype(bf16)

    proj = wt[...]
    proj = jnp.concatenate(
        [
            jnp.concatenate([proj, jnp.zeros_like(proj)], axis=1),
            jnp.concatenate([proj, -proj], axis=1),
        ],
        axis=0,
    )
    proj = jnp.concatenate([proj, proj], axis=1)
    vel[...] = jnp.dot(proj, attn[...], preferred_element_type=f32).T.astype(bf16)

    def rs_copy(d):
        to, seq = source(d)
        there = pl.ds(pl.multiple_of(OWN * seq, OWN), OWN)
        return remote(vel.at[there, :], rs.at[head], s_sum.at[0], r_sum.at[0], to)

    send_all(rs_copy, lambda: pltpu.make_async_copy(vel.at[rows, :], rs.at[head], r_sum.at[0]))
    await_bytes(rs, r_sum.at[0])

    mine = jnp.sum(rs[...].astype(f32), axis=0)
    turned = pltpu.roll(mine, LAT, 1)
    st[...] = jnp.concatenate(
        [jnp.sum(mine * mine, axis=0, keepdims=True), jnp.sum(mine * turned, axis=0, keepdims=True)], axis=0
    )

    @pl.loop(1, SEQ)
    def _(d):
        remote(st, ar1.at[s], s_sum.at[1], r_sum.at[1], along_seq(d)).start()

    pltpu.make_async_copy(st, ar1.at[s], r_sum.at[1]).start()
    await_bytes(ar1, r_sum.at[1])
    st2[...] = jnp.sum(ar1[...], axis=0)

    @pl.loop(1, 32)
    def _(g):
        remote(st2, ar2.at[w], s_sum.at[2], r_sum.at[2], along_win(g)).start()

    pltpu.make_async_copy(st2, ar2.at[w], r_sum.at[2]).start()
    await_bytes(ar2, r_sum.at[2])
    sums = jnp.sum(ar2[...], axis=0)
    is_cond = lax.broadcasted_iota(jnp.int32, (1, 2 * LAT), 1) < LAT
    s_cc = jnp.sum(jnp.where(is_cond, sums[0:1, :], 0.0), axis=1, keepdims=True)
    s_dd = jnp.sum(jnp.where(is_cond, 0.0, sums[0:1, :]), axis=1, keepdims=True)
    s_dc = jnp.sum(jnp.where(is_cond, sums[1:2, :], 0.0), axis=1, keepdims=True)
    clip_limit = clip_rms * math.sqrt(ROWS * WIN_COLS * LAT)
    clip_factor = jnp.minimum(1.0, clip_limit / jnp.sqrt(s_dd + tiny))
    along = s_dc / (s_cc + tiny)
    guided = mine + (guide_scale - 1.0) * clip_factor * (turned - along * mine)
    out_ref[...] = guided[:, :LAT]

    @pl.when(own_copy)
    def _():
        for copy in text_sends():
            copy.wait_send()
        most = pl.ds(0, SEQ - 1)
        await_bytes(stage.at[:, most], s_own.at[0])
        await_bytes(rs.at[most], s_sum.at[0])

    @pl.when(jnp.logical_not(own_copy))
    def _():
        await_bytes(stage, s_own.at[0])
        await_bytes(rs, s_sum.at[0])

    await_bytes(ar1.at[pl.ds(0, SEQ - 1)], s_sum.at[1])
    await_bytes(ar2.at[pl.ds(0, 31)], s_sum.at[2])
    @pl.loop(0, 9)
    def _(j):
        for n in range(2):
            await_bytes(kvd.at[0, n], s_sib.at[j, n])

        @pl.when(j > 0)
        def _():
            for n in range(2):
                await_bytes(kvd.at[0, n], s_blk.at[j, n])


def local(img_query, img_key, img_value, text_kv, vel_weight, window_px):
    dma = pltpu.SemaphoreType.DMA
    anywhere = pl.BlockSpec(memory_space=pl.ANY)
    out = pl.pallas_call(
        kernel,
        out_shape=jax.ShapeDtypeStruct((OWN, LAT), f32),
        in_specs=[anywhere] * 5 + [pl.BlockSpec(memory_space=pltpu.SMEM)],
        out_specs=pl.BlockSpec(memory_space=pltpu.VMEM),
        scratch_shapes=[
            pltpu.VMEM((3, 4, 4, HEADS * HD), bf16),
            pltpu.VMEM((3, HEADS, OWN, HD), bf16),
            pltpu.VMEM((9, 2, TOK, HD), bf16),
            pltpu.VMEM((9, 2, TOK, HD), bf16),
            pltpu.VMEM((TOK, HD), bf16),
            pltpu.VMEM((HD, TOK), bf16),
            pltpu.VMEM((2, 2, TXT, HD), bf16),
            pltpu.VMEM((LAT, HD), bf16),
            pltpu.VMEM((3, 19, HD, TOK), f32),
            pltpu.VMEM((3, 24, TOK), f32),
            pltpu.VMEM((3, 24, TOK), f32),
            pltpu.VMEM((2, HD, TOK), f32),
            pltpu.VMEM((2, 3, 24, TOK), f32),
            pltpu.VMEM((4 * HD, TOK), bf16),
            pltpu.VMEM((TOK, 2 * LAT), bf16),
            pltpu.VMEM((HEADS, OWN, 2 * LAT), bf16),
            pltpu.VMEM((2, 2 * LAT), f32),
            pltpu.VMEM((2, 2 * LAT), f32),
            pltpu.VMEM((SEQ, 2, 2 * LAT), f32),
            pltpu.VMEM((32, 2, 2 * LAT), f32),
            pltpu.SMEM((9,), jnp.int32),
            dma((3,)),
            dma((1,)),
            dma((3,)),
            dma((9, 2)),
            dma((9, 2)),
            dma((9, 2)),
            dma((9, 2)),
            dma((2,)),
            dma((2,)),
            dma((3,)),
            dma((3,)),
        ],
        compiler_params=pltpu.CompilerParams(
            collective_id=0, has_side_effects=True, vmem_limit_bytes=60 * 2**20
        ),
    )(img_query, img_key, img_value, text_kv, vel_weight.T, window_px)
    return out.reshape(4, 4, LAT)


def solution(mesh):
    in_specs = (
        P("win", "seq", None),
        P("win", "seq", None),
        P("win", "seq", None),
        P(None, None, None, "seq"),
        P("seq", None),
        P(),
    )
    out_specs = P("win", "seq", None)
    return jax.shard_map(local, mesh=mesh, in_specs=in_specs, out_specs=out_specs, check_vma=False)
```

time: 84.4 us -> 61.2 us (0.73)
  Pallas kernels: 77.1 us -> 59.7 us
  local copies, waits for them, and re-layouts: 6.84 us -> 1.3 us
    pallas_call x3 -> x1, Pallas kernels: 77.1 us -> 59.7 us  [local(): pl.pallas_call(kernel, out_shape=jax.ShapeDtypeStruct((OWN, LAT), f32), i...]
    unnamed x15 -> x1, local copies, waits for them, and re-layouts: 6.84 us -> 1.3 us
where the time goes in v2:
time: 61.2 us; the launch traced here: 61 us
  Pallas kernels  59.7 us (98%)
  local copies, waits for them, and re-layouts  1.3 us (2%)
    pallas_call x1, Pallas kernels, local(): pl.pallas_call(kernel, out_shape=jax.ShapeDtypeStruct((OWN, LAT), f32), i...  59.7 us
    unnamed x1, local copies, waits for them, and re-layouts  1.3 us

profile of v2, /device:TPU:1, one launch (start us, length us, event | category | flops | bytes accessed | tf_op | source)
XLA Modules:
  0.0 61.0 jit_solution(16105074546706826471)
XLA Ops:
  0.0 59.7 %shard_map.64 = f32[16,64]{1,0:T(8,128)} custom-call(bf16[4,4,2048]{2,1,0:T(4,128)(2,1)} %q_in.1, bf16[4,4,2048]{2,1,0:T(4,128)(2,1)} %k_in.1, bf16[4,4,2048]{2,1,0:T(4,128)(2,1)} %v_in.1, bf16[2,2,512,128]{3,2,1,0:T(8,128)(2,1)} %text_in.1, bf16[64,128]{1,0:T(8,128)(2,1)} %bitcast.3, s32[32]{0:T(128)} %px.1), custom_call_target="tpu_custom_call" | custom-call | tf_op jit(solution)/shard_map/pallas_call | solution.py:440
  59.7 1.3 %copy.8 = f32[4,4,64]{2,1,0:T(4,128)} copy(f32[4,4,64]{2,1,0:T(4,128)} %bitcast.2) | data formatting | bytes 8192

commit v3 on v2

--- a/solution.py
+++ b/solution.py
@@ -96,29 +96,31 @@
         def _(d):
             copy(d).start()
 
+    sibling = {"win": w, "seq": 2 * z + 1 - c}
+    up = {"win": 8 * x + 2 * mod(p + 1, 4) + a, "seq": s}
+    down = {"win": 8 * x + 2 * mod(p + 3, 4) + a, "seq": s}
+    barrier = pltpu.get_barrier_semaphore()
+
+    def hello(to):
+        pl.semaphore_signal(barrier, inc=1, device_id=to, device_id_type=MESH)
+
+    @pl.loop(1, SEQ)
+    def _(d):
+        hello(source(d)[0])
+
+    @pl.when(jnp.logical_not(own_copy))
+    def _():
+        hello(source(zero)[0])
+
+    hello(up)
+    hello(down)
+    hello({"win": 8 * mod(x + 1, 4) + y, "seq": s})
+    hello({"win": 8 * mod(x + 3, 4) + y, "seq": s})
+    hello(sibling)
+
     loads = [pltpu.make_async_copy(ref, raw.at[n], l_in.at[n]) for n, ref in enumerate((k_in, v_in, q_in))]
     for load in loads:
         load.start()
-
-    barrier = pltpu.get_barrier_semaphore()
-
-    def hello(to):
-        pl.semaphore_signal(barrier, inc=1, device_id=to, device_id_type=MESH)
-
-    @pl.loop(1, SEQ)
-    def _(d):
-        hello(dest(d)[0])
-        hello(source(d)[0])
-        hello(along_seq(d))
-
-    @pl.when(jnp.logical_not(own_copy))
-    def _():
-        hello(dest(zero)[0])
-        hello(source(zero)[0])
-
-    @pl.loop(1, 32)
-    def _(g):
-        hello(along_win(g))
 
     rows = pl.ds(pl.multiple_of(OWN * s, OWN), OWN)
     for n, load in enumerate(loads):
@@ -127,7 +129,7 @@
         for h in range(HEADS):
             stage[n, h] = flat[:, h * HD : (h + 1) * HD]
         if n == 0:
-            pl.semaphore_wait(barrier, jnp.where(own_copy, 3 * SEQ + 28, 3 * SEQ + 30))
+            pl.semaphore_wait(barrier, jnp.where(own_copy, SEQ + 4, SEQ + 5))
         dst = q_buf.at[rows, :] if n == 2 else kvd.at[0, n, rows, :]
 
         def give(d, n=n, dst=dst):
@@ -138,8 +140,6 @@
             return pltpu.make_async_copy(stage.at[n, head], dst, r_own.at[n])
 
         send_all(give, keep)
-
-    sibling = {"win": w, "seq": 2 * z + 1 - c}
 
     def text_sends():
         return (
@@ -163,17 +163,14 @@
         place = jnp.where(far, jnp.where(side == 1, place + 4, place - 4), place)
         return place
 
-    up = {"win": 8 * x + 2 * mod(p + 1, 4) + a, "seq": s}
-    down = {"win": 8 * x + 2 * mod(p + 3, 4) + a, "seq": s}
-
     def send_block(n, have, step, to):
-        remote(kvd.at[have, n], kvd.at[step, n], s_blk.at[step, n], r_blk.at[step, n], to).start()
+        remote(kvd.at[have, n], kvd.at[step, n], s_blk.at[0], r_blk.at[step, n], to).start()
 
     def send_x(n, have, step, side):
         send_block(n, have, step, {"win": 8 * mod(x + side, 4) + y, "seq": s})
 
     def send_sib(n, step):
-        remote(kvd.at[step, n], kvs.at[step, n], s_sib.at[step, n], r_sib.at[step, n], sibling).start()
+        remote(kvd.at[step, n], kvs.at[step, n], s_sib.at[0], r_sib.at[step], sibling).start()
 
     def hand_on(n, step, turn, x_step):
         await_bytes(kvd.at[step, n], r_blk.at[step, n])
@@ -191,11 +188,10 @@
     send_sib(0, 0)
     await_bytes(kvd.at[0, 1], r_own.at[1])
     send_block(1, 0, 2, down)
-    send_block(1, 0, 1, up)
-    send_block(0, 0, 2, down)
     send_x(1, 0, 4, 1)
     send_x(1, 0, 3, 3)
     send_sib(1, 0)
+
     def scan_start(n, found):
         start = div(px[n], 16)
         slot = div(start, 4)
@@ -294,10 +290,14 @@
 
         @pl.when(j == 0)
         def _():
+            send_block(1, 0, 1, up)
+            send_block(0, 0, 2, down)
+
+        @pl.when(j == 0)
+        def _():
             text_part()
 
-        for n in range(2):
-            await_bytes(kvs.at[j, n], r_sib.at[j, n])
+        await_bytes(kvs.at[j], r_sib.at[j])
         attend(kvs, j, 1 - c, place)
 
     query_row = mod(div(lax.broadcasted_iota(jnp.int32, (1, TOK), 1), 4), 4)
@@ -375,6 +375,21 @@
         return remote(vel.at[there, :], rs.at[head], s_sum.at[0], r_sum.at[0], to)
 
     send_all(rs_copy, lambda: pltpu.make_async_copy(vel.at[rows, :], rs.at[head], r_sum.at[0]))
+
+    @pl.when(own_copy)
+    def _():
+        for copy in text_sends():
+            copy.wait_send()
+        await_bytes(stage.at[:, pl.ds(0, SEQ - 1)], s_own.at[0])
+        await_bytes(rs.at[pl.ds(0, SEQ - 1)], s_sum.at[0])
+
+    @pl.when(jnp.logical_not(own_copy))
+    def _():
+        await_bytes(stage, s_own.at[0])
+        await_bytes(rs, s_sum.at[0])
+
+    await_bytes(kvd.at[pl.ds(0, 8)], s_blk.at[0])
+    await_bytes(kvd, s_sib.at[0])
     await_bytes(rs, r_sum.at[0])
 
     mine = jnp.sum(rs[...].astype(f32), axis=0)
@@ -407,31 +422,8 @@
     along = s_dc / (s_cc + tiny)
     guided = mine + (guide_scale - 1.0) * clip_factor * (turned - along * mine)
     out_ref[...] = guided[:, :LAT]
-
-    @pl.when(own_copy)
-    def _():
-        for copy in text_sends():
-            copy.wait_send()
-        most = pl.ds(0, SEQ - 1)
-        await_bytes(stage.at[:, most], s_own.at[0])
-        await_bytes(rs.at[most], s_sum.at[0])
-
-    @pl.when(jnp.logical_not(own_copy))
-    def _():
-        await_bytes(stage, s_own.at[0])
-        await_bytes(rs, s_sum.at[0])
-
     await_bytes(ar1.at[pl.ds(0, SEQ - 1)], s_sum.at[1])
     await_bytes(ar2.at[pl.ds(0, 31)], s_sum.at[2])
-    @pl.loop(0, 9)
-    def _(j):
-        for n in range(2):
-            await_bytes(kvd.at[0, n], s_sib.at[j, n])
-
-        @pl.when(j > 0)
-        def _():
-            for n in range(2):
-                await_bytes(kvd.at[0, n], s_blk.at[j, n])
 
 
 def local(img_query, img_key, img_value, text_kv, vel_weight, window_px):
@@ -467,10 +459,10 @@
             dma((3,)),
             dma((1,)),
             dma((3,)),
+            dma((1,)),
+            dma((1,)),
             dma((9, 2)),
-            dma((9, 2)),
-            dma((9, 2)),
-            dma((9, 2)),
+            dma((9,)),
             dma((2,)),
             dma((2,)),
             dma((3,)),

time: 61.2 us -> 59.3 us (0.969)
  Pallas kernels: 59.7 us -> 57.8 us
    pallas_call x1, Pallas kernels: 59.7 us -> 57.8 us  [local(): pl.pallas_call(kernel, out_shape=jax.ShapeDtypeStruct((OWN, LAT), f32), i...]
where the time goes in v3:
time: 59.3 us; the launch traced here: 59.1 us
  Pallas kernels  57.8 us (97%)
  local copies, waits for them, and re-layouts  1.3 us (2%)
    pallas_call x1, Pallas kernels, local(): pl.pallas_call(kernel, out_shape=jax.ShapeDtypeStruct((OWN, LAT), f32), i...  57.8 us
    unnamed x1, local copies, waits for them, and re-layouts  1.3 us

profile of v3, /device:TPU:1, one launch (start us, length us, event | category | flops | bytes accessed | tf_op | source)
XLA Modules:
  0.0 59.1 jit_solution(8333248023811941873)
XLA Ops:
  0.0 57.8 %shard_map.64 = f32[16,64]{1,0:T(8,128)} custom-call(bf16[4,4,2048]{2,1,0:T(4,128)(2,1)} %q_in.1, bf16[4,4,2048]{2,1,0:T(4,128)(2,1)} %k_in.1, bf16[4,4,2048]{2,1,0:T(4,128)(2,1)} %v_in.1, bf16[2,2,512,128]{3,2,1,0:T(8,128)(2,1)} %text_in.1, bf16[64,128]{1,0:T(8,128)(2,1)} %bitcast.3, s32[32]{0:T(128)} %px.1), custom_call_target="tpu_custom_call" | custom-call | tf_op jit(solution)/shard_map/pallas_call | solution.py:432
  57.8 1.3 %copy.8 = f32[4,4,64]{2,1,0:T(4,128)} copy(f32[4,4,64]{2,1,0:T(4,128)} %bitcast.2) | data formatting | bytes 8192

commit v4 on v3

--- a/solution.py
+++ b/solution.py
@@ -185,11 +185,11 @@
     send_block(0, 0, 1, up)
     send_x(0, 0, 4, 1)
     send_x(0, 0, 3, 3)
-    send_sib(0, 0)
     await_bytes(kvd.at[0, 1], r_own.at[1])
     send_block(1, 0, 2, down)
     send_x(1, 0, 4, 1)
     send_x(1, 0, 3, 3)
+    send_sib(0, 0)
     send_sib(1, 0)
 
     def scan_start(n, found):

time: 59.3 us -> 59.3 us (level)
  no operation moved by 1% of the time
where the time goes in v4:
time: 59.3 us; the launch traced here: 59.1 us
  Pallas kernels  57.8 us (97%)
  local copies, waits for them, and re-layouts  1.3 us (2%)
    pallas_call x1, Pallas kernels, local(): pl.pallas_call(kernel, out_shape=jax.ShapeDtypeStruct((OWN, LAT), f32), i...  57.8 us
    unnamed x1, local copies, waits for them, and re-layouts  1.3 us

profile of v4, /device:TPU:1, one launch (start us, length us, event | category | flops | bytes accessed | tf_op | source)
XLA Modules:
  0.0 59.1 jit_solution(13162073995635583978)
XLA Ops:
  0.0 57.8 %shard_map.64 = f32[16,64]{1,0:T(8,128)} custom-call(bf16[4,4,2048]{2,1,0:T(4,128)(2,1)} %q_in.1, bf16[4,4,2048]{2,1,0:T(4,128)(2,1)} %k_in.1, bf16[4,4,2048]{2,1,0:T(4,128)(2,1)} %v_in.1, bf16[2,2,512,128]{3,2,1,0:T(8,128)(2,1)} %text_in.1, bf16[64,128]{1,0:T(8,128)(2,1)} %bitcast.3, s32[32]{0:T(128)} %px.1), custom_call_target="tpu_custom_call" | custom-call | tf_op jit(solution)/shard_map/pallas_call | solution.py:432
  57.8 1.3 %copy.8 = f32[4,4,64]{2,1,0:T(4,128)} copy(f32[4,4,64]{2,1,0:T(4,128)} %bitcast.2) | data formatting | bytes 8192
